TPU v7x, 32 devices: a whole 2x2x4 slice. The times are simulated.
32 devices in a mesh: lon: 8 (over z, x), lat: 4 (over y, core).
Axes of the slice: x: 2, y: 2, z: 4, core: 2. Of those that a mesh axis runs over, the one named last changes fastest.
Arguments:
- elevation: float32 [12, 384, 1024], P(None, 'lat', 'lon'), may hold values from -6 to 6
- equilibrium: float32 [12, 384, 1024], P(None, 'lat', 'lon'), may hold values from -4 to 4
- transport_u: float32 [12, 384, 1024], P(None, 'lat', 'lon'), may hold values from -4 to 4
- transport_v: float32 [12, 384, 1024], P(None, 'lat', 'lon'), may hold values from -4 to 4
- ocean_depth: float32 [384, 1024], P('lat', 'lon'), may hold values from 0.3 to 3
- bottom_drag: float32 [384, 1024], P('lat', 'lon'), may hold values from 0.2 to 2
- wet_mask: int32 [384, 1024], P('lat', 'lon'), may hold values 0 or 1
- lon_green: float32 [1024, 128], P('lon'), may hold values from -0.5 to 0.5
- lat_green: float32 [384, 3072], P('lat', 'lon'), may hold values from -0.109375 to 0.109375
Outputs:
- elevation_next: float32 [12, 384, 1024], P(None, 'lat', 'lon')
- transport_u_next: float32 [12, 384, 1024], P(None, 'lat', 'lon')
- transport_v_next: float32 [12, 384, 1024], P(None, 'lat', 'lon')
All inputs are finite; a program needn't handle non-finite values. No bound on the sum of `wet_mask` on one device may be relied on, other than what follows from the above.
Results may differ from a plain program's by a relative error of at most 0.0001.
Values sent between devices are 32-bit elements; how exact they have to be, the bound alone decides.
A program may use at most 64 MiB of HBM per device.

v0:
```python
import math

import jax
import jax.numpy as jnp
from jax import lax
from jax.sharding import PartitionSpec as P

FREQS = [1.9323, 2.0, 1.896, 2.0055, 1.0027, 0.9295]
VISCOSITY = 0.5


def extended(array, sides, width, wrap):
    for axis, dim in sides:
        size, length = (lax.axis_size(axis), array.shape[dim])
        up = [(i, (i + 1) % size) for i in range(size if wrap else size - 1)]
        down = [(j, i) for i, j in up]
        last = lax.slice_in_dim(array, length - width, length, axis=dim)
        initial = lax.slice_in_dim(array, 0, width, axis=dim)
        before = lax.ppermute(last, axis, up)
        after = lax.ppermute(initial, axis, down)
        array = jnp.concatenate([before, array, after], axis=dim)
    return array


def row_terms(rows, nlat):
    angle = (-80.0 + 160.0 * (rows.astype(jnp.float32) + 0.5) / nlat) * (math.pi / 180.0)
    return ((1.0 / jnp.cos(angle))[:, None], (2.0 * jnp.sin(angle))[:, None])


def clipped_terms(first, count, nlat):
    rows = jnp.clip(first + jnp.arange(count), 0, nlat - 1)
    return row_terms(rows, nlat)


def extend(stack, width):
    widened = extended(stack, (("lon", 2),), width, True)
    return extended(widened, (("lat", 1),), width, False)


def slopes(potential_ext, stretch):
    east_slope = (potential_ext[:, 1:-1, 2:] - potential_ext[:, 1:-1, :-2]) * 0.5 * stretch
    north_slope = (potential_ext[:, 2:, 1:-1] - potential_ext[:, :-2, 1:-1]) * 0.5
    return (east_slope, north_slope)


def solve_cells(push_u, push_v, drag_field, wet_frac, coriolis):
    damping = drag_field + 4.0 * VISCOSITY
    frequency = jnp.array(FREQS, jnp.float32)[:, None, None]
    det_real = damping * damping - frequency * frequency + coriolis * coriolis
    det_imag = 2.0 * damping * frequency
    magnitude = det_real * det_real + det_imag * det_imag

    def combine(first, second, factor):
        top_real = damping * first[:6] - frequency * first[6:] + factor * coriolis * second[:6]
        top_imag = damping * first[6:] + frequency * first[:6] + factor * coriolis * second[6:]
        out_real = (top_real * det_real + top_imag * det_imag) / magnitude
        out_imag = (top_imag * det_real - top_real * det_imag) / magnitude
        return wet_frac * jnp.concatenate([out_real, out_imag], axis=0)

    return jnp.concatenate([combine(push_u, push_v, 1.0), combine(push_v, push_u, -1.0)], axis=0)


def relax(flow_ext, east_slope, north_slope, depth_field, drag_field, wet_frac, coriolis):
    beside_all = (
        flow_ext[:, :-2, 1:-1]
        + flow_ext[:, 2:, 1:-1]
        + flow_ext[:, 1:-1, :-2]
        + flow_ext[:, 1:-1, 2:]
    )
    push_u = -depth_field * east_slope + VISCOSITY * beside_all[:12]
    push_v = -depth_field * north_slope + VISCOSITY * beside_all[12:]
    return solve_cells(push_u, push_v, drag_field, wet_frac, coriolis)


def surface(east_ext, north_ext, stretch, wet_frac):
    spread = (east_ext[:, :, 2:] - east_ext[:, :, :-2]) * 0.5 * stretch + (
        north_ext[:, 2:, :] - north_ext[:, :-2, :]
    ) * 0.5
    frequency = jnp.array(FREQS, jnp.float32)[:, None, None]
    return wet_frac * jnp.concatenate([-spread[6:] / frequency, spread[:6] / frequency], axis=0)


def per_device(
    elevation,
    equilibrium,
    transport_u,
    transport_v,
    ocean_depth,
    bottom_drag,
    wet_mask,
    lon_green,
    lat_green,
):
    rows_here = elevation.shape[1]
    total_rows = rows_here * lax.axis_size("lat")
    wet_frac = wet_mask.astype(jnp.float32)
    source = wet_frac * elevation
    mixed = jnp.einsum("krj,cj->krc", source, lon_green, precision=lax.Precision.HIGHEST)
    sal = jnp.einsum(
        "rs,ksc->krc",
        lat_green,
        lax.all_gather(mixed, "lat", axis=1, tiled=True),
        precision=lax.Precision.HIGHEST,
    )
    potential = elevation - equilibrium - sal
    first_row = lax.axis_index("lat") * rows_here
    stretch, coriolis = row_terms(first_row + jnp.arange(rows_here), total_rows)
    flows = jnp.concatenate([transport_u, transport_v], axis=0)
    wide_flows = None
    stack = jnp.concatenate(
        [potential, flows, ocean_depth[None], bottom_drag[None], wet_frac[None]], axis=0
    )
    widened = extend(stack, 3)
    stretch_outer, coriolis_outer = clipped_terms(first_row - 2, rows_here + 4, total_rows)
    outer_statics = widened[36:39, 1:-1, 1:-1]
    inner_statics = widened[36:39, 2:-2, 2:-2]
    east_outer, north_outer = slopes(widened[:12], stretch_outer)
    middle = relax(
        widened[12:36],
        east_outer,
        north_outer,
        outer_statics[0],
        outer_statics[1],
        outer_statics[2],
        coriolis_outer,
    )
    wide_flows = relax(
        middle,
        east_outer[:, 1:-1, 1:-1],
        north_outer[:, 1:-1, 1:-1],
        inner_statics[0],
        inner_statics[1],
        inner_statics[2],
        coriolis_outer[1:-1],
    )
    flows = wide_flows[:, 1:-1, 1:-1]
    east_ext = wide_flows[:12, 1:-1, :]
    north_ext = wide_flows[12:, :, 1:-1]
    elevation_next = surface(east_ext, north_ext, stretch, wet_frac)
    return (elevation_next, flows[:12], flows[12:])


def solution(mesh):
    placed = (
        P(None, "lat", "lon"),
        P(None, "lat", "lon"),
        P(None, "lat", "lon"),
        P(None, "lat", "lon"),
        P("lat", "lon"),
        P("lat", "lon"),
        P("lat", "lon"),
        P("lon", None),
        P("lat", "lon"),
    )
    return jax.shard_map(
        per_device,
        mesh=mesh,
        in_specs=placed,
        out_specs=(P(None, "lat", "lon"), P(None, "lat", "lon"), P(None, "lat", "lon")),
        check_vma=False,
    )
```

profile of v0, /device:TPU:1, one launch (start us, length us, event | category | flops | bytes accessed | tf_op | source)
XLA Modules:
  0.0 95.1 jit_solution(13338213882671567967)
XLA Ops:
  7.2 0.0 copy-start
  7.2 0.0 copy-start.3
  7.2 0.0 all-gather.2.cloned.1.call-start
  7.2 0.9 convert_element_type.28
  8.1 2.5 %fusion.45 = f32[12,96,128]{2,1,0:T(8,128)} fusion(f32[12,96,128]{2,1,0:T(8,128)} %param.12, f32[96,128]{1,0:T(8,128)S(1)} %convert_element_type.28, f32[128,128]{1,0:T(8,128)} %param.19), kind=kOutput, calls=%fused_computation.92 | convolution fusion | flops 226639872 | bytes 1294336 | tf_op jit(solution)/shard_map/krj,cj->krc/dot_general | solution.py:98
  10.6 0.0 all-gather.2.cloned.1.call-update
  10.7 0.1 broadcast_multiply_fusion.2
  10.8 0.1 fusion.59
  10.8 0.0 copy-start.4
  10.8 26.5 %all-gather.2.cloned.1.call-done = f32[12,384,128]{2,1,0:T(8,128)} async-done(((f32[12,96,128]{2,1,0:T(8,128)}), f32[12,384,128]{2,1,0:T(8,128)}) %all-gather.2.cloned.1.call-update) | async-done | bytes 2359312 | tf_op jit(solution)/shard_map/all_gather | solution.py:102
  37.4 0.0 copy-done
  37.4 0.0 copy-done.3
  37.4 0.0 copy-start.5
  37.4 3.5 %fusion.13 = f32[39,96,128]{2,1,0:T(8,128)S(1)} fusion(f32[12,384,128]{2,1,0:T(8,128)} %all-gather.2.cloned.1.call-done, f32[12,96,128]{2,1,0:T(8,128)S(1)} %copy-done.3, f32[12,96,128]{2,1,0:T(8,128)} %param.13, f32[96,384]{1,0:T(8,128)S(1)} %copy-done), kind=kOutput, calls=%fused_computation.47 | convolution fusion | flops 679772160 | bytes 4276224 | tf_op jit(solution)/shard_map/rs,ksc->krc/dot_general | solution.py:99
  40.8 0.0 copy-done.4
  40.9 0.0 copy-start.7
  40.9 0.0 copy-start.8
  40.9 0.0 copy-start.6
  40.9 0.0 copy-done.5
  41.0 0.7 copy-done.7
  41.7 0.0 copy-done.8
  41.7 0.0 copy-done.6
  41.7 2.5 %fusion.57 = (f32[39,96,3]{2,1,0:T(8,128)}, f32[39,96,3]{2,1,0:T(8,128)}) fusion(f32[39,96,128]{2,1,0:T(8,128)S(1)} %bitcast_dynamic-update-slice_fusion), kind=kLoop, calls=%fused_computation.130 | loop fusion | bytes 179712 | tf_op jit(solution)/shard_map/slice | solution.py:17
  44.2 2.1 %copy.15 = f32[39,96,3]{1,0,2:T(8,128)S(1)} copy(f32[39,96,3]{2,1,0:T(8,128)} %get-tuple-element.42) | data formatting | bytes 89856 | tf_op jit(solution)/shard_map/slice | solution.py:17
  46.3 2.1 %copy.16 = f32[39,96,3]{1,0,2:T(8,128)S(1)} copy(f32[39,96,3]{2,1,0:T(8,128)} %get-tuple-element.43) | data formatting | bytes 89856 | tf_op jit(solution)/shard_map/slice | solution.py:18
  48.5 4.0 %collective-permute-start.1 = (f32[39,96,3]{1,0,2:T(8,128)S(1)}, f32[39,96,3]{1,0,2:T(8,128)S(1)}, u32[]{:S(2)}, u32[]{:S(2)}) collective-permute-start(f32[39,96,3]{1,0,2:T(8,128)S(1)} %copy.16), channel_id=1, source_target_pairs={{4,0},{8,4},{12,8},{16,12},{20,16},{24,20},{28,24},{0,28},{5,1},{9... | collective-permute-start | bytes 134792 | tf_op jit(solution)/shard_map/ppermute | solution.py:20
  52.5 0.0 collective-permute-start
  52.5 0.1 fusion.54
  52.5 5.7 %collective-permute-done = f32[39,96,3]{1,0,2:T(8,128)S(1)} collective-permute-done((f32[39,96,3]{1,0,2:T(8,128)S(1)}, f32[39,96,3]{1,0,2:T(8,128)S(1)}, u32[]{:S(2)}, u32[]{:S(2)}) %collective-permute-start) | collective-permute-done | bytes 44960 | tf_op jit(solution)/shard_map/ppermute | solution.py:19
  58.2 1.9 %copy.17 = f32[39,96,3]{2,1,0:T(8,128)} copy(f32[39,96,3]{1,0,2:T(8,128)S(1)} %collective-permute-done) | data formatting | bytes 89856 | tf_op jit(solution)/shard_map/ppermute | solution.py:19
  60.1 0.0 collective-permute-done.1
  60.1 1.9 %copy.18 = f32[39,96,3]{2,1,0:T(8,128)} copy(f32[39,96,3]{1,0,2:T(8,128)S(1)} %collective-permute-done.1) | data formatting | bytes 89856 | tf_op jit(solution)/shard_map/ppermute | solution.py:20
  62.0 0.0 copy-start.1
  62.0 1.6 %pad_maximum_fusion.4 = (f32[39,3,134]{2,1,0:T(4,128)S(1)}, f32[39,3,134]{2,1,0:T(4,128)S(1)}) fusion(f32[39,96,3]{2,1,0:T(8,128)} %copy.18, f32[39,96,128]{2,1,0:T(8,128)S(1)} %bitcast_dynamic-update-slice_fusion, f32[39,96,3]{2,1,0:T(8,128)} %copy.17), kind=kLoop, calls=%fused_computation.100 | loop fusion | flops 62712 | bytes 2132208 | tf_op jit(solution)/shard_map/slice | solution.py:17
  63.7 3.8 %collective-permute-start.2 = (f32[39,3,134]{2,1,0:T(4,128)S(1)}, f32[39,3,134]{2,1,0:T(4,128)S(1)}, u32[]{:S(2)}, u32[]{:S(2)}) collective-permute-start(f32[39,3,134]{2,1,0:T(4,128)S(1)} %get-tuple-element.32), channel_id=1, source_target_pairs={{0,1},{1,2},{2,3},{4,5},{5,6},{6,7},{8,9},{9,10},{10,11},{12,13},{... | collective-permute-start | bytes 188144 | tf_op jit(solution)/shard_map/ppermute | solution.py:19
  67.4 2.1 %collective-permute-start.3 = (f32[39,3,134]{2,1,0:T(4,128)S(1)}, f32[39,3,134]{2,1,0:T(4,128)S(1)}, u32[]{:S(2)}, u32[]{:S(2)}) collective-permute-start(f32[39,3,134]{2,1,0:T(4,128)S(1)} %get-tuple-element.33), channel_id=1, source_target_pairs={{1,0},{2,1},{3,2},{5,4},{6,5},{7,6},{9,8},{10,9},{11,10},{13,12},{... | collective-permute-start | bytes 188144 | tf_op jit(solution)/shard_map/ppermute | solution.py:20
  69.5 0.1 divide_multiply_fusion.1
  69.6 0.0 collective-permute-done.2
  69.6 4.4 %collective-permute-done.3 = f32[39,3,134]{2,1,0:T(4,128)S(1)} collective-permute-done((f32[39,3,134]{2,1,0:T(4,128)S(1)}, f32[39,3,134]{2,1,0:T(4,128)S(1)}, u32[]{:S(2)}, u32[]{:S(2)}) %collective-permute-start.3) | collective-permute-done | bytes 62744 | tf_op jit(solution)/shard_map/ppermute | solution.py:20
  74.0 0.0 copy-done.1
  74.0 0.0 copy-done.2
  74.0 0.2 multiply_bitcast_fusion.3
  74.2 0.2 maximum_bitcast_fusion.1
  74.5 1.8 %pad_maximum_fusion = f32[39,102,134]{2,1,0:T(8,128)S(1)} fusion(f32[39,3,134]{2,1,0:T(4,128)S(1)} %collective-permute-done.3, f32[39,96,3]{2,1,0:T(8,128)S(1)} %copy-done.2, f32[39,96,128]{2,1,0:T(8,128)S(1)} %bitcast_dynamic-update-slice_fusion, f32[39,96,3]{2,1,0:T(8,128)S(1)} %copy-done.1, f32[39,3,134]{2,1,0:T(4,128)S(1)} %collective-permute-done.2), kind=kLoop, calls=%fused_computation | loop fusion | flops 2132208 | bytes 4264416 | tf_op jit(solution)/shard_map/concatenate | solution.py:21
  76.3 2.1 %slice_add_fusion = f32[24,100,132]{2,1,0:T(8,128)S(1)} fusion(f32[39,102,134]{2,1,0:T(8,128)S(1)} %pad_maximum_fusion), kind=kLoop, calls=%fused_computation.14 | loop fusion | flops 950400 | bytes 6336000 | tf_op jit(solution)/shard_map/add | solution.py:65
  78.4 0.1 broadcast_multiply_fusion
  78.5 0.0 copy-start.9
  78.5 0.0 copy-start.10
  78.5 1.2 %fusion.10 = (f32[12,100,132]{2,1,0:T(8,128)S(1)}, f32[12,100,132]{2,1,0:T(8,128)S(1)}, f32[12,100,132]{2,1,0:T(8,128)S(1)}, f32[12,100,132]{2,1,0:T(8,128)S(1)}) fusion(f32[24,100,132]{2,1,0:T(8,128)S(1)} %slice_add_fusion, f32[100,132]{1,0:T(8,128)S(1)} %get-tuple-element.24, f32[100]{0:T(128)S(1)} %divide_multiply_fusion.1, ...), kind=kLoop, calls=%fused_computation.37 | loop fusion | flops 1425600 | bytes 6442000 | tf_op jit(solution)/shard_map/add | solution.py:70
  79.7 0.0 copy-done.9
  79.7 0.0 copy-done.10
  79.7 0.8 fusion.20
  80.5 0.4 fusion.22
  81.0 0.2 maximum_multiply_fusion.1
  81.1 2.1 %fusion.2 = f32[24,98,130]{2,1,0:T(8,128)S(1)} fusion(f32[12,100,132]{2,1,0:T(8,128)S(1)} %get-tuple-element.56, f32[12,100,132]{2,1,0:T(8,128)S(1)} %get-tuple-element.55), kind=kLoop, calls=%fused_computation.9 | loop fusion | flops 2140320 | bytes 2490240 | tf_op jit(solution)/shard_map/add | solution.py:65
  83.2 0.8 fusion.6
  84.0 0.8 fusion.24
  84.8 0.4 fusion.27
  85.2 0.2 maximum_multiply_fusion.2
  85.4 0.0 copy-start.11
  85.5 1.9 %fusion.58 = (f32[12,96,128]{2,1,0:T(8,128)}, f32[12,96,128]{2,1,0:T(8,128)S(1)}, f32[12,96,128]{2,1,0:T(8,128)}) fusion(f32[12,98,130]{2,1,0:T(8,128)S(1)} %get-tuple-element.54, f32[96]{0:T(128)S(1)} %divide_multiply_fusion, f32[12,98,130]{2,1,0:T(8,128)S(1)} %get-tuple-element.53), kind=kLoop, calls=%fused_computation.131 | loop fusion | flops 737280 | bytes 5308800 | tf_op jit(solution)/shard_map/slice | solution.py:140
  87.3 0.0 copy-done.11
  87.3 0.1 fusion.47
  87.4 0.9 maximum_multiply_fusion.4
  (9 shorter events, 0.2 us)
Async XLA Ops:
  7.2 30.2 %copy-start = (f32[96,384]{1,0:T(8,128)S(1)}, f32[96,384]{1,0:T(8,128)}, u32[]{:S(2)}) copy-start(f32[96,384]{1,0:T(8,128)} %param.20) | copy-start | bytes 442372
  7.2 30.2 %copy-start.3 = (f32[12,96,128]{2,1,0:T(8,128)S(1)}, f32[12,96,128]{2,1,0:T(8,128)}, u32[]{:S(2)}) copy-start(f32[12,96,128]{2,1,0:T(8,128)} %param.12) | copy-start | bytes 1769476
  7.2 30.2 %all-gather.2.cloned.1.call-start = ((), (), s32[]{:S(2)}) async-start(), calls=%async_computation | async-start | bytes 2949120 | tf_op jit(solution)/shard_map/all_gather | solution.py:102
  10.8 30.0 %copy-start.4 = (f32[12,96,128]{2,1,0:T(8,128)S(1)}, f32[12,96,128]{2,1,0:T(8,128)}, u32[]{:S(2)}) copy-start(f32[12,96,128]{2,1,0:T(8,128)} %param.14) | copy-start | bytes 1769476
  37.4 3.6 %copy-start.5 = (f32[12,96,128]{2,1,0:T(8,128)S(1)}, f32[12,96,128]{2,1,0:T(8,128)}, u32[]{:S(2)}) copy-start(f32[12,96,128]{2,1,0:T(8,128)} %param.15) | copy-start | bytes 1769476
  40.9 0.8 copy-start.7
  40.9 0.8 copy-start.8
  40.9 0.8 copy-start.6
  48.5 11.6 %collective-permute-start.1 = (f32[39,96,3]{1,0,2:T(8,128)S(1)}, f32[39,96,3]{1,0,2:T(8,128)S(1)}, u32[]{:S(2)}, u32[]{:S(2)}) collective-permute-start(f32[39,96,3]{1,0,2:T(8,128)S(1)} %copy.16), channel_id=1, source_target_pairs={{4,0},{8,4},{12,8},{16,12},{20,16},{24,20},{28,24},{0,28},{5,1},{9... | collective-permute-start | bytes 134792 | tf_op jit(solution)/shard_map/ppermute | solution.py:20
  52.5 5.8 %collective-permute-start = (f32[39,96,3]{1,0,2:T(8,128)S(1)}, f32[39,96,3]{1,0,2:T(8,128)S(1)}, u32[]{:S(2)}, u32[]{:S(2)}) collective-permute-start(f32[39,96,3]{1,0,2:T(8,128)S(1)} %copy.15), channel_id=1, source_target_pairs={{0,4},{4,8},{8,12},{12,16},{16,20},{20,24},{24,28},{28,0},{1,5},{5... | collective-permute-start | bytes 134792 | tf_op jit(solution)/shard_map/ppermute | solution.py:19
  62.0 12.0 %copy-start.1 = (f32[39,96,3]{2,1,0:T(8,128)S(1)}, f32[39,96,3]{2,1,0:T(8,128)}, u32[]{:S(2)}) copy-start(f32[39,96,3]{2,1,0:T(8,128)} %copy.17) | copy-start | bytes 134788
  62.0 12.0 %copy-start.2 = (f32[39,96,3]{2,1,0:T(8,128)S(1)}, f32[39,96,3]{2,1,0:T(8,128)}, u32[]{:S(2)}) copy-start(f32[39,96,3]{2,1,0:T(8,128)} %copy.18) | copy-start | bytes 134788
  63.7 6.0 %collective-permute-start.2 = (f32[39,3,134]{2,1,0:T(4,128)S(1)}, f32[39,3,134]{2,1,0:T(4,128)S(1)}, u32[]{:S(2)}, u32[]{:S(2)}) collective-permute-start(f32[39,3,134]{2,1,0:T(4,128)S(1)} %get-tuple-element.32), channel_id=1, source_target_pairs={{0,1},{1,2},{2,3},{4,5},{5,6},{6,7},{8,9},{9,10},{10,11},{12,13},{... | collective-permute-start | bytes 188144 | tf_op jit(solution)/shard_map/ppermute | solution.py:19
  67.4 6.6 %collective-permute-start.3 = (f32[39,3,134]{2,1,0:T(4,128)S(1)}, f32[39,3,134]{2,1,0:T(4,128)S(1)}, u32[]{:S(2)}, u32[]{:S(2)}) collective-permute-start(f32[39,3,134]{2,1,0:T(4,128)S(1)} %get-tuple-element.33), channel_id=1, source_target_pairs={{1,0},{2,1},{3,2},{5,4},{6,5},{7,6},{9,8},{10,9},{11,10},{13,12},{... | collective-permute-start | bytes 188144 | tf_op jit(solution)/shard_map/ppermute | solution.py:20
  78.5 1.2 %copy-start.9 = (f32[6]{0:T(128)S(1)}, f32[6]{0:T(128)}, u32[]{:S(2)}) copy-start(f32[6]{0:T(128)} %constant.56) | copy-start | bytes 76
  78.5 1.2 %copy-start.10 = (f32[6]{0:T(128)S(1)}, f32[6]{0:T(128)}, u32[]{:S(2)}) copy-start(f32[6]{0:T(128)} %constant.12.clone) | copy-start | bytes 76
  85.4 1.9 %copy-start.11 = (f32[6]{0:T(128)S(1)}, f32[6]{0:T(128)}, u32[]{:S(2)}) copy-start(f32[6]{0:T(128)} %constant.13) | copy-start | bytes 76
Sparse Core Ops, SparseCore 0:
  10.8 26.5 all-gather.1
where the time goes:
time: 95.4 us; the launch traced here: 95.1 us
  waiting for transfers between devices  36.7 us (38%)
  other arithmetic  16.9 us (18%)
  between operations  14.3 us (15%)
  local copies, waits for them, and re-layouts  11.4 us (12%)
  starting transfers between devices  9.89 us (10%)
  matrix products  5.99 us (6%)
    all_gather x1, waiting for transfers between devices, per_device(): lax.all_gather(mixed, 'lat', axis=1, tiled=True)  26.5 us
    ppermute x2, starting transfers between devices, extended(): after = lax.ppermute(initial, axis, down)  6.08 us
    ppermute x2, waiting for transfers between devices, extended(): before = lax.ppermute(last, axis, up)  5.75 us
    slice x2, local copies, waits for them, and re-layouts, extended(): last = lax.slice_in_dim(array, length - width, length, axis=dim)  4.63 us
    ppermute x2, waiting for transfers between devices, extended(): after = lax.ppermute(initial, axis, down)  4.4 us
    add x2, other arithmetic, relax(): flow_ext[:, :-2, 1:-1] + flow_ext[:, 2:, 1:-1] + flow_ext[:, 1:-1, :-2]  4.14 us
    ppermute x2, starting transfers between devices, extended(): before = lax.ppermute(last, axis, up)  3.77 us
    dot_general x1, matrix products, per_device(): jnp.einsum('rs,ksc->krc', lat_green, lax.all_gather(mixed, 'lat', axis=1,...  3.47 us
  transfers between devices with their start and end apart: 5, of which 3 were waited for; matrix products, arithmetic and copies ran while one was open for 2% of the time, Pallas kernels for 0%

commit v1 on v0

v1 whole, which is shorter than its diff:
```python
import functools
import math

import jax
import jax.numpy as jnp
from jax import lax
from jax.experimental import pallas as pl
from jax.experimental.pallas import tpu as pltpu
from jax.sharding import PartitionSpec as P

FREQS = [1.9323, 2.0, 1.896, 2.0055, 1.0027, 0.9295]
MESH = pl.DeviceIdType.MESH
HIGH = lax.Precision.HIGHEST
TOP = 16
HALO = 8
BLOCK = 16
STATICS = (36, 37, 38)
FIELDS = tuple(range(24)) + STATICS


def freq_of(j):
    w = jnp.float32(FREQS[0])
    for i in range(1, 6):
        w = jnp.where(j == i, jnp.float32(FREQS[i]), w)
    return w


def kernel(
    n_lat, n_lon, rows,
    elev_h, equil_h, u_h, v_h, dep_h, drag_h, mask_h, lon_h, lat_h,
    oe_h, ou_h, ov_h,
    elev_v, equil_v, mask_v, lon_v, lg, f, fs, mid, mids, two, twos, co, cos, tt, g,
    geo, x0, zl0, zr0, xp, zlp, zrp, eo,
    load_sem, g_send, g_recv, f_send, f_recv, a_send, a_recv, b_send, b_recv, p_send, p_recv, o_sem,
):
    total = n_lat * rows
    end = TOP + rows
    lo, hi = TOP - HALO, end + HALO
    blocks = (hi - lo) // BLOCK
    lat = lax.axis_index("lat")
    lon = lax.axis_index("lon")
    core, chip = lax.rem(lat, 2), lat // 2
    chips = n_lat // 2
    sib = lat + 1 - 2 * core
    right, left = lax.rem(lon + 1, n_lon), lax.rem(lon + n_lon - 1, n_lon)

    loads = [
        (elev_h, elev_v), (mask_h, mask_v), (equil_h, equil_v),
        (u_h, f.at[0:12, TOP:end]), (v_h, f.at[12:24, TOP:end]),
        (dep_h, f.at[36, TOP:end]), (drag_h, f.at[37, TOP:end]),
        (lat_h, lg.at[TOP:end]), (lon_h, lon_v),
    ]
    loads = [pltpu.make_async_copy(s, d, load_sem.at[i]) for i, (s, d) in enumerate(loads)]
    for c in loads:
        c.start()

    barrier = pltpu.get_barrier_semaphore()
    for d in range(1, n_lat):
        pl.semaphore_signal(barrier, inc=1, device_id={"lat": lax.rem(lat + d, n_lat)}, device_id_type=MESH)
    for side in (left, right):
        pl.semaphore_signal(barrier, inc=1, device_id={"lon": side}, device_id_type=MESH)

    own = pl.ds(pl.multiple_of(lat * rows, 8), rows)
    loads[0].wait()
    loads[1].wait()
    f[38, TOP:end] = mask_v[...].astype(jnp.float32)

    def make_source(j, _):
        wet = f[38, TOP:end]
        g[j, own, 0:128] = wet * elev_v[j]
        g[j, own, 128:256] = wet * elev_v[j + 6]
        return 0

    lax.fori_loop(0, 6, make_source, 0)
    pl.semaphore_wait(barrier, n_lat + 1)

    def remote(src, dst, ss, rs, where):
        return pltpu.make_async_remote_copy(
            src_ref=src, dst_ref=dst, send_sem=ss, recv_sem=rs, device_id=where, device_id_type=MESH)

    def block_of(d):
        return pl.ds(pl.multiple_of((lax.rem(chip + chips - d, chips) * 2 + core) * rows, 8), rows)

    def gather_copy(j, d):
        where = sib if d == 0 else lax.rem(chip + d, chips) * 2 + core
        return remote(g.at[j, own], g.at[j, own], g_send.at[j, d], g_recv.at[j, d], {"lat": where})

    def forward_copy(j, d):
        rows_d = block_of(d)
        return remote(g.at[j, rows_d], g.at[j, rows_d], f_send.at[j, d - 1], f_recv.at[j, d - 1], {"lat": sib})

    def start_gather(j, _):
        for d in range(1, chips):
            gather_copy(j, d).start()
        gather_copy(j, 0).start()
        return 0

    lax.fori_loop(0, 2, start_gather, 0)

    for c in loads[2:]:
        c.wait()

    def make_gap(k, _):
        f[24 + k, TOP:end] = elev_v[k] - equil_v[k]
        return 0

    lax.fori_loop(0, 12, make_gap, 0)

    up = [remote(f.at[:, TOP:TOP + HALO], f.at[:, end:hi], a_send.at[0], a_recv.at[0], {"lat": lax.max(lat - 1, 0)}),
          remote(lg.at[TOP:TOP + HALO], lg.at[end:hi], a_send.at[1], a_recv.at[1], {"lat": lax.max(lat - 1, 0)})]
    down = [remote(f.at[:, end - HALO:end], f.at[:, lo:TOP], a_send.at[2], a_recv.at[2], {"lat": lax.min(lat + 1, n_lat - 1)}),
            remote(lg.at[end - HALO:end], lg.at[lo:TOP], a_send.at[3], a_recv.at[3], {"lat": lax.min(lat + 1, n_lat - 1)})]

    @pl.when(lat > 0)
    def _():
        for c in up:
            c.start()

    @pl.when(lat < n_lat - 1)
    def _():
        for c in down:
            c.start()

    lax.fori_loop(2, 6, start_gather, 0)

    @pl.when(lat == 0)
    def _():
        f[:, lo:TOP] = jnp.zeros((39, HALO, 128), jnp.float32)
        lg[lo:TOP] = jnp.zeros((HALO, total), jnp.float32)

    @pl.when(lat == n_lat - 1)
    def _():
        f[:, end:hi] = jnp.zeros((39, HALO, 128), jnp.float32)
        lg[end:hi] = jnp.zeros((HALO, total), jnp.float32)

    row = lax.broadcasted_iota(jnp.int32, (hi + HALO, 128), 0) + (lat * rows - TOP)
    angle = (-80.0 + 160.0 * (row.astype(jnp.float32) + 0.5) / total) * (math.pi / 180.0)
    geo[0] = 1.0 / jnp.cos(angle)
    geo[1] = 2.0 * jnp.sin(angle)

    @pl.when(lat > 0)
    def _():
        for c in up:
            c.wait_send()
        for c in down:
            c.wait_recv()

    @pl.when(lat < n_lat - 1)
    def _():
        for c in down:
            c.wait_send()
        for c in up:
            c.wait_recv()

    lane = lax.broadcasted_iota(jnp.int32, (BLOCK, 128), 1)
    shifted = lax.rem(lane + 124, 128)
    window = shifted // 8
    from_left = lax.rem(shifted, 8) < 4

    def pack(pieces):
        packed = jnp.zeros((BLOCK, 128), jnp.float32)
        for pos, piece in enumerate(pieces):
            shift = (8 * pos + 8) % 128
            rolled = pltpu.roll(piece, shift, 1) if shift else piece
            packed = jnp.where(window == pos, rolled, packed)
        return packed

    def unpack(z, pos):
        shift = (128 - (8 * pos + 8)) % 128
        return pltpu.roll(z, shift, 1) if shift else z

    slots = [(fi, b) for fi in FIELDS for b in range(blocks)]
    tiles = -(-len(slots) // 16)
    for t in range(tiles):
        part = slots[16 * t:16 * t + 16]
        x0[t] = pack([f[fi, lo + BLOCK * b:lo + BLOCK * b + BLOCK] for fi, b in part])
    edge = [remote(x0, zl0, b_send.at[0], b_recv.at[0], {"lon": right}),
            remote(x0, zr0, b_send.at[1], b_recv.at[1], {"lon": left})]
    for c in edge:
        c.start()

    def coefficients(fields, coefs, j):
        w = freq_of(j)
        for b in range(blocks):
            rs = slice(lo + BLOCK * b, lo + BLOCK * b + BLOCK)
            d = fields[37, rs] + 2.0
            c = geo[1, rs]
            det_r = d * d - w * w + c * c
            det_i = 2.0 * d * w
            inv = fields[38, rs] * 0.5 / (det_r * det_r + det_i * det_i)
            coefs[4 * j, rs] = (d * det_r + w * det_i) * inv
            coefs[4 * j + 1, rs] = (w * det_r - d * det_i) * inv
            coefs[4 * j + 2, rs] = c * det_r * inv
            coefs[4 * j + 3, rs] = -c * det_i * inv

    def coef_main(j, _):
        coefficients(f, co, j)
        return 0

    def coef_side(j, _):
        coefficients(fs, cos, j)
        return 0

    lax.fori_loop(0, 6, coef_main, 0)
    for c in edge:
        c.wait()
    for t in range(tiles):
        z = jnp.where(from_left, zl0[t], zr0[t])
        for pos, (fi, b) in enumerate(slots[16 * t:16 * t + 16]):
            fs[fi, lo + BLOCK * b:lo + BLOCK * b + BLOCK] = unpack(z, pos)
    lax.fori_loop(0, 6, coef_side, 0)

    first_lane, last_lane = lane == 0, lane == 127

    def strips(j):
        return [remote(xp.at[j], zlp.at[j], p_send.at[j, 0], p_recv.at[j, 0], {"lon": right}),
                remote(xp.at[j], zrp.at[j], p_send.at[j, 1], p_recv.at[j, 1], {"lon": left})]

    def outs(j):
        copies = []
        for part in range(2):
            k = j + 6 * part
            copies += [
                pltpu.make_async_copy(eo.at[k], oe_h.at[k], o_sem.at[j, 3 * part]),
                pltpu.make_async_copy(two.at[k, TOP:end], ou_h.at[k], o_sem.at[j, 3 * part + 1]),
                pltpu.make_async_copy(two.at[12 + k, TOP:end], ov_h.at[k], o_sem.at[j, 3 * part + 2]),
            ]
        return copies

    def loading(j):
        for d in range(1, chips):
            gather_copy(j, d).wait_recv()
            forward_copy(j, d).start()
        gather_copy(j, 0).wait_recv()
        for d in range(1, chips):
            forward_copy(j, d).wait_recv()
        both = jnp.dot(lg[lo:hi], g[j], precision=HIGH, preferred_element_type=jnp.float32)
        for part in range(2):
            k = 24 + j + 6 * part
            sal = lax.dot_general(
                both[:, 128 * part:128 * part + 128], lon_v[...], (((1,), (1,)), ((), ())),
                precision=HIGH, preferred_element_type=jnp.float32)
            f[k, lo:hi] = f[k, lo:hi] - sal
        xp[j] = pack([
            f[24 + j + 6 * part, lo + BLOCK * b:lo + BLOCK * b + BLOCK]
            for part in range(2) for b in range(blocks)])
        for c in strips(j):
            c.start()

    def east_west(m, s):
        em, es = pltpu.roll(m, 127, 1), pltpu.roll(s, 127, 1)
        wm, ws = pltpu.roll(m, 1, 1), pltpu.roll(s, 1, 1)
        return (jnp.where(last_lane, es, em), jnp.where(last_lane, em, es),
                jnp.where(first_lane, ws, wm), jnp.where(first_lane, wm, ws))

    def relax(src, srcs, dst, dsts, j, b, side_v):
        r0 = lo + BLOCK * b
        rs, rn, ro = slice(r0, r0 + BLOCK), slice(r0 + 1, r0 + 1 + BLOCK), slice(r0 - 1, r0 - 1 + BLOCK)
        pm, ps = [], []
        for i in range(4):
            k = j + 6 * i
            em, es, wm, ws = east_west(src[k, rs], srcs[k, rs])
            pm.append(tt[i, rs] + (em + wm + src[k, rn] + src[k, ro]))
            ps.append(tt[4 + i, rs] + (es + ws + srcs[k, rn] + srcs[k, ro]))
        for push, coefs, to, with_v in ((pm, co, dst, True), (ps, cos, dsts, side_v)):
            ar, ai, br, bi = (coefs[4 * j + i, rs] for i in range(4))
            ur, ui, vr, vi = push
            to[j, rs] = ar * ur - ai * ui + br * vr - bi * vi
            to[j + 6, rs] = ar * ui + ai * ur + br * vi + bi * vr
            if with_v:
                to[j + 12, rs] = ar * vr - ai * vi - br * ur + bi * ui
                to[j + 18, rs] = ar * vi + ai * vr - br * ui - bi * ur

    def finish(j):
        for c in strips(j):
            c.wait()
        z = jnp.where(from_left, zlp[j], zrp[j])
        for part in range(2):
            for b in range(blocks):
                fs[24 + j + 6 * part, lo + BLOCK * b:lo + BLOCK * b + BLOCK] = unpack(z, part * blocks + b)
        for b in range(blocks):
            r0 = lo + BLOCK * b
            rs, rn, ro = slice(r0, r0 + BLOCK), slice(r0 + 1, r0 + 1 + BLOCK), slice(r0 - 1, r0 - 1 + BLOCK)
            stretch = geo[0, rs]
            dm, ds = f[36, rs], fs[36, rs]
            for part in range(2):
                k = 24 + j + 6 * part
                em, es, wm, ws = east_west(f[k, rs], fs[k, rs])
                tt[part, rs] = dm * stretch * (wm - em)
                tt[4 + part, rs] = ds * stretch * (ws - es)
                tt[2 + part, rs] = dm * (f[k, ro] - f[k, rn])
                tt[6 + part, rs] = ds * (fs[k, ro] - fs[k, rn])
        for b in range(blocks):
            relax(f, fs, mid, mids, j, b, True)
        for b in range(blocks):
            relax(mid, mids, two, twos, j, b, False)
        scale = 0.5 / freq_of(j)
        for b in range(rows // BLOCK):
            r0 = TOP + BLOCK * b
            rs, rn, ro = slice(r0, r0 + BLOCK), slice(r0 + 1, r0 + 1 + BLOCK), slice(r0 - 1, r0 - 1 + BLOCK)
            stretch = geo[0, rs]
            wet = f[38, rs] * scale
            spread = []
            for part in range(2):
                k = j + 6 * part
                em, _, wm, _ = east_west(two[k, rs], twos[k, rs])
                spread.append((em - wm) * stretch + (two[12 + k, rn] - two[12 + k, ro]))
            eo[j, BLOCK * b:BLOCK * b + BLOCK] = -wet * spread[1]
            eo[j + 6, BLOCK * b:BLOCK * b + BLOCK] = wet * spread[0]
        for c in outs(j):
            c.start()

    def step(j, _):
        @pl.when(j < 6)
        def _():
            loading(lax.min(j, 5))

        @pl.when(j > 0)
        def _():
            finish(lax.max(j - 1, 0))

        return 0

    lax.fori_loop(0, 7, step, 0)

    def drain(j, _):
        for c in outs(j):
            c.wait()
        for d in range(chips):
            gather_copy(j, d).wait_send()
        for d in range(1, chips):
            forward_copy(j, d).wait_send()
        return 0

    lax.fori_loop(0, 6, drain, 0)


def solution(mesh):
    n_lat, n_lon = mesh.shape["lat"], mesh.shape["lon"]

    def per_device(*args):
        rows = args[0].shape[1]
        total = n_lat * rows
        ext = rows + 2 * TOP
        blocks = (rows + 2 * HALO) // BLOCK
        tiles = -(-len(FIELDS) * blocks // 16)
        chips = n_lat // 2
        vmem = lambda *shape: pltpu.VMEM(shape, jnp.float32)
        dma = lambda *shape: pltpu.SemaphoreType.DMA(shape)
        out = jax.ShapeDtypeStruct((12, rows, 128), jnp.float32)
        return tuple(pl.pallas_call(
            functools.partial(kernel, n_lat, n_lon, rows),
            out_shape=[out] * 3,
            in_specs=[pl.BlockSpec(memory_space=pl.ANY)] * 9,
            out_specs=[pl.BlockSpec(memory_space=pl.ANY)] * 3,
            scratch_shapes=[
                vmem(12, rows, 128), vmem(12, rows, 128), pltpu.VMEM((rows, 128), jnp.int32), vmem(128, 128),
                vmem(ext, total), vmem(39, ext, 128), vmem(39, ext, 128), vmem(24, ext, 128), vmem(24, ext, 128),
                vmem(24, ext, 128), vmem(24, ext, 128), vmem(24, ext, 128), vmem(24, ext, 128),
                vmem(8, ext, 128), vmem(6, total, 256), vmem(2, ext, 128),
                vmem(tiles, BLOCK, 128), vmem(tiles, BLOCK, 128), vmem(tiles, BLOCK, 128),
                vmem(6, BLOCK, 128), vmem(6, BLOCK, 128), vmem(6, BLOCK, 128), vmem(12, rows, 128),
                dma(9), dma(6, chips), dma(6, chips), dma(6, chips - 1), dma(6, chips - 1),
                dma(4), dma(4), dma(2), dma(2), dma(6, 2), dma(6, 2), dma(6, 6),
            ],
            compiler_params=pltpu.CompilerParams(
                collective_id=0, has_side_effects=True, vmem_limit_bytes=50 * 1024 * 1024),
            cost_estimate=pl.CostEstimate(flops=1_000_000_000, bytes_accessed=6_000_000, transcendentals=0),
        )(*args))

    placed = (P(None, "lat", "lon"),) * 4 + (P("lat", "lon"),) * 3 + (P("lon", None), P("lat", "lon"))
    return jax.shard_map(
        per_device, mesh=mesh, in_specs=placed, out_specs=(P(None, "lat", "lon"),) * 3, check_vma=False)
```

time: 95.4 us -> 59.1 us (0.62)
  the two profiles are of different devices: /device:TPU:1 before, /device:TPU:0 now
where the time goes in v1:
time: 59.1 us; the launch traced here: 58.6 us
  Pallas kernels  48.2 us (82%)
  local copies, waits for them, and re-layouts  9.77 us (17%)
  between operations  0.66 us (1%)
    pallas_call x1, Pallas kernels, per_device(): pl.pallas_call(functools.partial(kernel, n_lat, n_lon, rows), out_shape=[...  48.2 us
    unnamed x19, local copies, waits for them, and re-layouts  9.77 us

profile of v1, /device:TPU:0, one launch (start us, length us, event | category | flops | bytes accessed | tf_op | source)
XLA Modules:
  0.0 58.6 jit_solution(16065267314690862067)
XLA Ops:
  0.6 0.0 copy-start
  0.6 1.1 %copy-done = f32[12,96,128]{2,1,0:T(8,128)S(1)} copy-done((f32[12,96,128]{2,1,0:T(8,128)S(1)}, f32[12,96,128]{2,1,0:T(8,128)}, u32[]{:S(2)}) %copy-start) | copy-done | bytes 589848
  1.7 0.0 copy-start.1
  1.7 1.1 %copy-done.1 = f32[12,96,128]{2,1,0:T(8,128)S(1)} copy-done((f32[12,96,128]{2,1,0:T(8,128)S(1)}, f32[12,96,128]{2,1,0:T(8,128)}, u32[]{:S(2)}) %copy-start.1) | copy-done | bytes 589848
  2.8 0.0 copy-start.2
  2.8 1.1 %copy-done.2 = f32[12,96,128]{2,1,0:T(8,128)S(1)} copy-done((f32[12,96,128]{2,1,0:T(8,128)S(1)}, f32[12,96,128]{2,1,0:T(8,128)}, u32[]{:S(2)}) %copy-start.2) | copy-done | bytes 589848
  3.8 0.0 copy-start.3
  3.8 0.9 %copy-done.3 = f32[96,384]{1,0:T(8,128)S(1)} copy-done((f32[96,384]{1,0:T(8,128)S(1)}, f32[96,384]{1,0:T(8,128)}, u32[]{:S(2)}) %copy-start.3) | copy-done | bytes 147480
  4.7 0.0 copy-start.4
  4.7 0.8 %copy-done.4 = f32[128,128]{1,0:T(8,128)S(1)} copy-done((f32[128,128]{1,0:T(8,128)S(1)}, f32[128,128]{1,0:T(8,128)}, u32[]{:S(2)}) %copy-start.4) | copy-done | bytes 65560
  5.6 0.0 copy-start.5
  5.6 0.8 %copy-done.5 = f32[96,128]{1,0:T(8,128)S(1)} copy-done((f32[96,128]{1,0:T(8,128)S(1)}, f32[96,128]{1,0:T(8,128)}, u32[]{:S(2)}) %copy-start.5) | copy-done | bytes 49176
  6.4 0.0 copy-start.6
  6.4 0.8 %copy-done.6 = f32[96,128]{1,0:T(8,128)S(1)} copy-done((f32[96,128]{1,0:T(8,128)S(1)}, f32[96,128]{1,0:T(8,128)}, u32[]{:S(2)}) %copy-start.6) | copy-done | bytes 49176
  7.2 0.0 copy-start.7
  7.2 0.8 %copy-done.7 = s32[96,128]{1,0:T(8,128)S(1)} copy-done((s32[96,128]{1,0:T(8,128)S(1)}, s32[96,128]{1,0:T(8,128)}, u32[]{:S(2)}) %copy-start.7) | copy-done | bytes 49176
  8.0 48.2 %shard_map.112 = (f32[12,96,128]{2,1,0:T(8,128)S(1)}, f32[12,96,128]{2,1,0:T(8,128)S(1)}, f32[12,96,128]{2,1,0:T(8,128)S(1)}) custom-call(f32[12,96,128]{2,1,0:T(8,128)S(1)} %copy-done, f32[12,96,128]{2,1,0:T(8,128)S(1)} %copy-done.1, f32[12,96,128]{2,1,0:T(8,128)S(1)} %copy-done.2, f32[12,96,128]{2,1,0:T(8,128)} %v_h.1, f32[96,128]{1,0:T(8,128)S(1)} %copy-done.5, ...), custom_call_target="tpu_custom_call" | custom-call | flops 1000000000 | bytes 6000000 | tf_op jit(solution)/shard_map/pallas_call | solution.py:351
  56.1 0.8 %copy.15 = f32[12,96,128]{2,1,0:T(8,128)} copy(f32[12,96,128]{2,1,0:T(8,128)S(1)} %get-tuple-element.6) | data formatting | bytes 1179648
  57.0 0.8 %copy.16 = f32[12,96,128]{2,1,0:T(8,128)} copy(f32[12,96,128]{2,1,0:T(8,128)S(1)} %get-tuple-element.7) | data formatting | bytes 1179648
  57.8 0.8 %copy.17 = f32[12,96,128]{2,1,0:T(8,128)} copy(f32[12,96,128]{2,1,0:T(8,128)S(1)} %get-tuple-element.8) | data formatting | bytes 1179648
Async XLA Ops:
  0.6 1.1 %copy-start = (f32[12,96,128]{2,1,0:T(8,128)S(1)}, f32[12,96,128]{2,1,0:T(8,128)}, u32[]{:S(2)}) copy-start(f32[12,96,128]{2,1,0:T(8,128)} %elev_h.1) | copy-start | bytes 1769476
  1.7 1.1 %copy-start.1 = (f32[12,96,128]{2,1,0:T(8,128)S(1)}, f32[12,96,128]{2,1,0:T(8,128)}, u32[]{:S(2)}) copy-start(f32[12,96,128]{2,1,0:T(8,128)} %equil_h.1) | copy-start | bytes 1769476
  2.8 1.1 %copy-start.2 = (f32[12,96,128]{2,1,0:T(8,128)S(1)}, f32[12,96,128]{2,1,0:T(8,128)}, u32[]{:S(2)}) copy-start(f32[12,96,128]{2,1,0:T(8,128)} %u_h.1) | copy-start | bytes 1769476
  3.8 0.9 %copy-start.3 = (f32[96,384]{1,0:T(8,128)S(1)}, f32[96,384]{1,0:T(8,128)}, u32[]{:S(2)}) copy-start(f32[96,384]{1,0:T(8,128)} %lat_h.1) | copy-start | bytes 442372
  4.7 0.8 %copy-start.4 = (f32[128,128]{1,0:T(8,128)S(1)}, f32[128,128]{1,0:T(8,128)}, u32[]{:S(2)}) copy-start(f32[128,128]{1,0:T(8,128)} %lon_h.1) | copy-start | bytes 196612
  5.6 0.8 %copy-start.5 = (f32[96,128]{1,0:T(8,128)S(1)}, f32[96,128]{1,0:T(8,128)}, u32[]{:S(2)}) copy-start(f32[96,128]{1,0:T(8,128)} %dep_h.1) | copy-start | bytes 147460
  6.4 0.8 %copy-start.6 = (f32[96,128]{1,0:T(8,128)S(1)}, f32[96,128]{1,0:T(8,128)}, u32[]{:S(2)}) copy-start(f32[96,128]{1,0:T(8,128)} %drag_h.1) | copy-start | bytes 147460
  7.2 0.8 %copy-start.7 = (s32[96,128]{1,0:T(8,128)S(1)}, s32[96,128]{1,0:T(8,128)}, u32[]{:S(2)}) copy-start(s32[96,128]{1,0:T(8,128)} %mask_h.1) | copy-start | bytes 147460

commit v2 on v1

--- a/solution.py
+++ b/solution.py
@@ -13,6 +13,7 @@
 HIGH = lax.Precision.HIGHEST
 TOP = 16
 HALO = 8
+SENT = 4
 BLOCK = 16
 STATICS = (36, 37, 38)
 FIELDS = tuple(range(24)) + STATICS
@@ -72,6 +73,15 @@
         return 0
 
     lax.fori_loop(0, 6, make_source, 0)
+    for c in loads[2:]:
+        c.wait()
+
+    def make_gap(k, _):
+        f[24 + k, TOP:end] = elev_v[k] - equil_v[k]
+        return 0
+
+    lax.fori_loop(0, 12, make_gap, 0)
+
     pl.semaphore_wait(barrier, n_lat + 1)
 
     def remote(src, dst, ss, rs, where):
@@ -95,21 +105,10 @@
         gather_copy(j, 0).start()
         return 0
 
-    lax.fori_loop(0, 2, start_gather, 0)
-
-    for c in loads[2:]:
-        c.wait()
-
-    def make_gap(k, _):
-        f[24 + k, TOP:end] = elev_v[k] - equil_v[k]
-        return 0
-
-    lax.fori_loop(0, 12, make_gap, 0)
-
-    up = [remote(f.at[:, TOP:TOP + HALO], f.at[:, end:hi], a_send.at[0], a_recv.at[0], {"lat": lax.max(lat - 1, 0)}),
-          remote(lg.at[TOP:TOP + HALO], lg.at[end:hi], a_send.at[1], a_recv.at[1], {"lat": lax.max(lat - 1, 0)})]
-    down = [remote(f.at[:, end - HALO:end], f.at[:, lo:TOP], a_send.at[2], a_recv.at[2], {"lat": lax.min(lat + 1, n_lat - 1)}),
-            remote(lg.at[end - HALO:end], lg.at[lo:TOP], a_send.at[3], a_recv.at[3], {"lat": lax.min(lat + 1, n_lat - 1)})]
+    up = [remote(f.at[:, TOP:TOP + SENT], f.at[:, end:end + SENT], a_send.at[0], a_recv.at[0], {"lat": lax.max(lat - 1, 0)}),
+          remote(lg.at[TOP:TOP + SENT], lg.at[end:end + SENT], a_send.at[1], a_recv.at[1], {"lat": lax.max(lat - 1, 0)})]
+    down = [remote(f.at[:, end - SENT:end], f.at[:, TOP - SENT:TOP], a_send.at[2], a_recv.at[2], {"lat": lax.min(lat + 1, n_lat - 1)}),
+            remote(lg.at[end - SENT:end], lg.at[TOP - SENT:TOP], a_send.at[3], a_recv.at[3], {"lat": lax.min(lat + 1, n_lat - 1)})]
 
     @pl.when(lat > 0)
     def _():
@@ -121,7 +120,7 @@
         for c in down:
             c.start()
 
-    lax.fori_loop(2, 6, start_gather, 0)
+    lax.fori_loop(0, 6, start_gather, 0)
 
     @pl.when(lat == 0)
     def _():
@@ -202,14 +201,6 @@
         return 0
 
     lax.fori_loop(0, 6, coef_main, 0)
-    for c in edge:
-        c.wait()
-    for t in range(tiles):
-        z = jnp.where(from_left, zl0[t], zr0[t])
-        for pos, (fi, b) in enumerate(slots[16 * t:16 * t + 16]):
-            fs[fi, lo + BLOCK * b:lo + BLOCK * b + BLOCK] = unpack(z, pos)
-    lax.fori_loop(0, 6, coef_side, 0)
-
     first_lane, last_lane = lane == 0, lane == 127
 
     def strips(j):
@@ -227,10 +218,12 @@
             ]
         return copies
 
-    def loading(j):
+    def passing(j):
         for d in range(1, chips):
             gather_copy(j, d).wait_recv()
             forward_copy(j, d).start()
+
+    def loading(j):
         gather_copy(j, 0).wait_recv()
         for d in range(1, chips):
             forward_copy(j, d).wait_recv()
@@ -310,18 +303,34 @@
         for c in outs(j):
             c.start()
 
+    passing(0)
+    passing(1)
+    loading(0)
+    loading(1)
+    for c in edge:
+        c.wait()
+    for t in range(tiles):
+        z = jnp.where(from_left, zl0[t], zr0[t])
+        for pos, (fi, b) in enumerate(slots[16 * t:16 * t + 16]):
+            fs[fi, lo + BLOCK * b:lo + BLOCK * b + BLOCK] = unpack(z, pos)
+    lax.fori_loop(0, 6, coef_side, 0)
+
     def step(j, _):
         @pl.when(j < 6)
         def _():
-            loading(lax.min(j, 5))
-
-        @pl.when(j > 0)
+            passing(lax.min(j, 5))
+
+        @pl.when(jnp.logical_and(j > 2, j < 7))
         def _():
-            finish(lax.max(j - 1, 0))
-
-        return 0
-
-    lax.fori_loop(0, 7, step, 0)
+            loading(lax.max(lax.min(j - 1, 5), 0))
+
+        @pl.when(j > 2)
+        def _():
+            finish(lax.max(j - 3, 0))
+
+        return 0
+
+    lax.fori_loop(2, 9, step, 0)
 
     def drain(j, _):
         for c in outs(j):
@@ -351,8 +360,8 @@
         return tuple(pl.pallas_call(
             functools.partial(kernel, n_lat, n_lon, rows),
             out_shape=[out] * 3,
-            in_specs=[pl.BlockSpec(memory_space=pl.ANY)] * 9,
-            out_specs=[pl.BlockSpec(memory_space=pl.ANY)] * 3,
+            in_specs=[pl.BlockSpec(memory_space=pltpu.HBM)] * 9,
+            out_specs=[pl.BlockSpec(memory_space=pltpu.HBM)] * 3,
             scratch_shapes=[
                 vmem(12, rows, 128), vmem(12, rows, 128), pltpu.VMEM((rows, 128), jnp.int32), vmem(128, 128),
                 vmem(ext, total), vmem(39, ext, 128), vmem(39, ext, 128), vmem(24, ext, 128), vmem(24, ext, 128),
@@ -364,7 +373,7 @@
                 dma(4), dma(4), dma(2), dma(2), dma(6, 2), dma(6, 2), dma(6, 6),
             ],
             compiler_params=pltpu.CompilerParams(
-                collective_id=0, has_side_effects=True, vmem_limit_bytes=50 * 1024 * 1024),
+                collective_id=0, has_side_effects=True, vmem_limit_bytes=62 * 1024 * 1024),
             cost_estimate=pl.CostEstimate(flops=1_000_000_000, bytes_accessed=6_000_000, transcendentals=0),
         )(*args))
 

time: 59.1 us -> 38 us (0.64)
  Pallas kernels: 48.2 us -> 33 us
  local copies, waits for them, and re-layouts: 9.77 us -> 4.07 us
    pallas_call x1, Pallas kernels: 48.2 us -> 33 us  [per_device(): pl.pallas_call(functools.partial(kernel, n_lat, n_lon, rows), out_shape=[...]
    unnamed x19 -> x7, local copies, waits for them, and re-layouts: 9.77 us -> 4.07 us
where the time goes in v2:
time: 38 us; the launch traced here: 37.7 us
  Pallas kernels  33 us (87%)
  local copies, waits for them, and re-layouts  4.07 us (11%)
  between operations  0.65 us (2%)
    pallas_call x1, Pallas kernels, per_device(): pl.pallas_call(functools.partial(kernel, n_lat, n_lon, rows), out_shape=[...  33 us
    unnamed x7, local copies, waits for them, and re-layouts  4.07 us

profile of v2, /device:TPU:0, one launch (start us, length us, event | category | flops | bytes accessed | tf_op | source)
XLA Modules:
  0.0 37.7 jit_solution(14311523056949753510)
XLA Ops:
  0.6 33.0 %shard_map.112 = (f32[12,96,128]{2,1,0:T(8,128)}, f32[12,96,128]{2,1,0:T(8,128)}, f32[12,96,128]{2,1,0:T(8,128)}) custom-call(f32[12,96,128]{2,1,0:T(8,128)} %elev_h.1, f32[12,96,128]{2,1,0:T(8,128)} %equil_h.1, f32[12,96,128]{2,1,0:T(8,128)} %u_h.1, f32[12,96,128]{2,1,0:T(8,128)} %v_h.1, f32[96,128]{1,0:T(8,128)} %dep_h.1, f32[96,128]{1,0:T(8,128)} %drag_h.1, ...), custom_call_target="tpu_custom_call" | custom-call | flops 1000000000 | bytes 6000000 | tf_op jit(solution)/shard_map/pallas_call | solution.py:360
  33.7 0.0 copy-start.1
  33.7 2.0 %copy.15 = f32[12,96,128]{2,1,0:T(8,128)} copy(f32[12,96,128]{2,1,0:T(8,128)} %get-tuple-element.6) | data formatting | bytes 1179648
  35.7 0.0 copy-done.1
  35.7 0.0 copy-start
  35.7 0.8 %copy.16 = f32[12,96,128]{2,1,0:T(8,128)} copy(f32[12,96,128]{2,1,0:T(8,128)S(1)} %copy-done.1) | data formatting | bytes 1179648
  36.5 0.5 %copy-done = f32[12,96,128]{2,1,0:T(8,128)S(1)} copy-done((f32[12,96,128]{2,1,0:T(8,128)S(1)}, f32[12,96,128]{2,1,0:T(8,128)}, u32[]{:S(2)}) %copy-start) | copy-done | bytes 589848
  36.9 0.8 %copy.17 = f32[12,96,128]{2,1,0:T(8,128)} copy(f32[12,96,128]{2,1,0:T(8,128)S(1)} %copy-done) | data formatting | bytes 1179648
Async XLA Ops:
  33.7 2.0 %copy-start.1 = (f32[12,96,128]{2,1,0:T(8,128)S(1)}, f32[12,96,128]{2,1,0:T(8,128)}, u32[]{:S(2)}) copy-start(f32[12,96,128]{2,1,0:T(8,128)} %get-tuple-element.7) | copy-start | bytes 1769476
  35.7 1.3 %copy-start = (f32[12,96,128]{2,1,0:T(8,128)S(1)}, f32[12,96,128]{2,1,0:T(8,128)}, u32[]{:S(2)}) copy-start(f32[12,96,128]{2,1,0:T(8,128)} %get-tuple-element.8) | copy-start | bytes 1769476

commit v3 on v2

--- a/solution.py
+++ b/solution.py
@@ -357,11 +357,12 @@
         vmem = lambda *shape: pltpu.VMEM(shape, jnp.float32)
         dma = lambda *shape: pltpu.SemaphoreType.DMA(shape)
         out = jax.ShapeDtypeStruct((12, rows, 128), jnp.float32)
+        args = [pltpu.with_memory_space_constraint(a, pltpu.HBM) for a in args]
         return tuple(pl.pallas_call(
             functools.partial(kernel, n_lat, n_lon, rows),
             out_shape=[out] * 3,
             in_specs=[pl.BlockSpec(memory_space=pltpu.HBM)] * 9,
-            out_specs=[pl.BlockSpec(memory_space=pltpu.HBM)] * 3,
+            out_specs=[pl.BlockSpec(memory_space=pl.ANY)] * 3,
             scratch_shapes=[
                 vmem(12, rows, 128), vmem(12, rows, 128), pltpu.VMEM((rows, 128), jnp.int32), vmem(128, 128),
                 vmem(ext, total), vmem(39, ext, 128), vmem(39, ext, 128), vmem(24, ext, 128), vmem(24, ext, 128),
@@ -373,7 +374,7 @@
                 dma(4), dma(4), dma(2), dma(2), dma(6, 2), dma(6, 2), dma(6, 6),
             ],
             compiler_params=pltpu.CompilerParams(
-                collective_id=0, has_side_effects=True, vmem_limit_bytes=62 * 1024 * 1024),
+                collective_id=0, has_side_effects=True, vmem_limit_bytes=48 * 1024 * 1024),
             cost_estimate=pl.CostEstimate(flops=1_000_000_000, bytes_accessed=6_000_000, transcendentals=0),
         )(*args))
 

time: 38 us -> 36.9 us (0.971)
  local copies, waits for them, and re-layouts: 4.07 us -> 2.45 us
  Pallas kernels: 33 us -> 33.6 us
    unnamed x7 -> x3, local copies, waits for them, and re-layouts: 4.07 us -> 2.45 us
    pallas_call x1, Pallas kernels: 33 us -> 33.6 us  [per_device(): pl.pallas_call(functools.partial(kernel, n_lat, n_lon, rows), out_shape=[...]
where the time goes in v3:
time: 36.9 us; the launch traced here: 36.7 us
  Pallas kernels  33.6 us (91%)
  local copies, waits for them, and re-layouts  2.45 us (7%)
  between operations  0.64 us (2%)
    pallas_call x1, Pallas kernels, per_device(): pl.pallas_call(functools.partial(kernel, n_lat, n_lon, rows), out_shape=[...  33.6 us
    unnamed x3, local copies, waits for them, and re-layouts  2.45 us

profile of v3, /device:TPU:0, one launch (start us, length us, event | category | flops | bytes accessed | tf_op | source)
XLA Modules:
  0.0 36.7 jit_solution(2529510919433556893)
XLA Ops:
  0.6 33.6 %shard_map.112 = (f32[12,96,128]{2,1,0:T(8,128)S(1)}, f32[12,96,128]{2,1,0:T(8,128)S(1)}, f32[12,96,128]{2,1,0:T(8,128)S(1)}) custom-call(f32[12,96,128]{2,1,0:T(8,128)} %elev_h.1, f32[12,96,128]{2,1,0:T(8,128)} %equil_h.1, f32[12,96,128]{2,1,0:T(8,128)} %u_h.1, f32[12,96,128]{2,1,0:T(8,128)} %v_h.1, f32[96,128]{1,0:T(8,128)} %dep_h.1, f32[96,128]{1,0:T(8,128)} %drag_h.1, ...), custom_call_target="tpu_custom_call" | custom-call | flops 1000000000 | bytes 6000000 | tf_op jit(solution)/shard_map/pallas_call | solution.py:361
  34.3 0.8 %copy.15 = f32[12,96,128]{2,1,0:T(8,128)} copy(f32[12,96,128]{2,1,0:T(8,128)S(1)} %get-tuple-element.6) | data formatting | bytes 1179648
  35.1 0.8 %copy.16 = f32[12,96,128]{2,1,0:T(8,128)} copy(f32[12,96,128]{2,1,0:T(8,128)S(1)} %get-tuple-element.7) | data formatting | bytes 1179648
  35.9 0.8 %copy.17 = f32[12,96,128]{2,1,0:T(8,128)} copy(f32[12,96,128]{2,1,0:T(8,128)S(1)} %get-tuple-element.8) | data formatting | bytes 1179648

commit v4 on v3

--- a/solution.py
+++ b/solution.py
@@ -324,13 +324,13 @@
         def _():
             loading(lax.max(lax.min(j - 1, 5), 0))
 
-        @pl.when(j > 2)
+        @pl.when(jnp.logical_or(jnp.logical_and(j > 2, j < 5), j > 5))
         def _():
-            finish(lax.max(j - 3, 0))
-
-        return 0
-
-    lax.fori_loop(2, 9, step, 0)
+            finish(lax.max(j - 3 - j // 5, 0))
+
+        return 0
+
+    lax.fori_loop(2, 10, step, 0)
 
     def drain(j, _):
         for c in outs(j):

time: 36.9 us -> 35.8 us (0.970)
  Pallas kernels: 33.6 us -> 32.6 us
    pallas_call x1, Pallas kernels: 33.6 us -> 32.6 us  [per_device(): pl.pallas_call(functools.partial(kernel, n_lat, n_lon, rows), out_shape=[...]
where the time goes in v4:
time: 35.8 us; the launch traced here: 35.7 us
  Pallas kernels  32.6 us (91%)
  local copies, waits for them, and re-layouts  2.45 us (7%)
  between operations  0.64 us (2%)
    pallas_call x1, Pallas kernels, per_device(): pl.pallas_call(functools.partial(kernel, n_lat, n_lon, rows), out_shape=[...  32.6 us
    unnamed x3, local copies, waits for them, and re-layouts  2.45 us

profile of v4, /device:TPU:0, one launch (start us, length us, event | category | flops | bytes accessed | tf_op | source)
XLA Modules:
  0.0 35.7 jit_solution(466551510675540305)
XLA Ops:
  0.6 32.6 %shard_map.112 = (f32[12,96,128]{2,1,0:T(8,128)S(1)}, f32[12,96,128]{2,1,0:T(8,128)S(1)}, f32[12,96,128]{2,1,0:T(8,128)S(1)}) custom-call(f32[12,96,128]{2,1,0:T(8,128)} %elev_h.1, f32[12,96,128]{2,1,0:T(8,128)} %equil_h.1, f32[12,96,128]{2,1,0:T(8,128)} %u_h.1, f32[12,96,128]{2,1,0:T(8,128)} %v_h.1, f32[96,128]{1,0:T(8,128)} %dep_h.1, f32[96,128]{1,0:T(8,128)} %drag_h.1, ...), custom_call_target="tpu_custom_call" | custom-call | flops 1000000000 | bytes 6000000 | tf_op jit(solution)/shard_map/pallas_call | solution.py:361
  33.2 0.8 %copy.15 = f32[12,96,128]{2,1,0:T(8,128)} copy(f32[12,96,128]{2,1,0:T(8,128)S(1)} %get-tuple-element.6) | data formatting | bytes 1179648
  34.1 0.8 %copy.16 = f32[12,96,128]{2,1,0:T(8,128)} copy(f32[12,96,128]{2,1,0:T(8,128)S(1)} %get-tuple-element.7) | data formatting | bytes 1179648
  34.9 0.8 %copy.17 = f32[12,96,128]{2,1,0:T(8,128)} copy(f32[12,96,128]{2,1,0:T(8,128)S(1)} %get-tuple-element.8) | data formatting | bytes 1179648
